TPU v7x, 256 devices: a whole 4x4x8 slice. The times are simulated.
256 devices in a mesh: ta: 4 (over x), col: 4 (over z_hi), vert: 16 (over y, z_lo, core).
Axes of the slice: x: 4, y: 4, z: 8 (z_hi: 4, z_lo: 2; z = z_hi * 2 + z_lo), core: 2. Of those that a mesh axis runs over, the one named last changes fastest.
Arguments:
- voltages: bfloat16 [4096, 262144], P(('vert', 'col'), 'ta'), may hold values from -6 to 6
- taps: float32 [4, 16384], replicated, may hold values from -3 to 3
- channels: int32 [16], replicated, may hold values from 0 to 8191
Outputs:
- visibilities: bfloat16 [16, 2, 4096, 4096], P('col', None, 'vert', 'ta')
Inputs may be any that keep to these rules, and one draw needn't show every extreme that they name: `channels`: channel numbers of the subset, possibly repeated.
All inputs are finite; a program needn't handle non-finite values.
Results may differ from a plain program's by a relative error of at most 0.0057.
Values may be sent and summed in bfloat16 or wider, within the bound.
No kernel may reach another device: no remote copies, remote signals or barrier semaphores. Data moves between devices by JAX's collectives and lax.ppermute only.
A program may use at most 192 MiB of HBM per device.

v0:
```python
import math

import jax
import jax.numpy as jnp
from jax import lax
from jax.sharding import PartitionSpec as P


def passed_along(shard, axis, by):
    peers = lax.axis_size(axis)
    pairs = [(i, i + by) for i in range(peers) if 0 <= i + by < peers]
    return lax.ppermute(shard, axis, pairs)


def dft_table(channels, length):
    index = lax.broadcasted_iota(jnp.int32, (length, channels.shape[0]), 0)
    phase = index * channels[None, :] % length
    angle = phase.astype(jnp.float32) * (2.0 * math.pi / length)
    scale = 1.0 / math.sqrt(length)
    return jnp.concatenate([jnp.cos(angle), -jnp.sin(angle)], axis=1) * scale


def correlate(rows, cols):
    count = rows.shape[0]
    depth = rows.shape[2]
    left = rows.reshape(count, 2 * depth, rows.shape[3])
    right_real = cols.reshape(count, 2 * depth, cols.shape[3])
    right_imag = jnp.concatenate([-cols[:, 1], cols[:, 0]], axis=1)
    right = jnp.concatenate([right_real, right_imag], axis=2)
    product = jnp.einsum("cpr,cpq->crq", left, right, preferred_element_type=jnp.float32)
    product = product.reshape(count, rows.shape[3], 2, cols.shape[3])
    return jnp.transpose(product, (0, 2, 1, 3))


def shards(voltages, taps, channels):
    inputs_dev = voltages.shape[0]
    frame_len = taps.shape[1]
    tap_count = taps.shape[0]
    lag = tap_count - 1
    spec_dev = voltages.shape[1] // frame_len
    chan_count = channels.shape[0]
    frames = voltages.reshape(inputs_dev, spec_dev, frame_len)
    table = dft_table(channels, frame_len)
    previous = passed_along(frames[:, spec_dev - lag :], "ta", 1)
    extended = jnp.concatenate([previous, frames], axis=1)
    filtered = jnp.zeros((inputs_dev, spec_dev, frame_len), jnp.float32)
    for tap in range(tap_count):
        filtered = filtered + taps[tap][None, None, :] * extended[:, tap : tap + spec_dev].astype(
            jnp.float32
        )
    result = jnp.dot(
        filtered.reshape(-1, frame_len),
        table,
        precision=lax.Precision.HIGHEST,
        preferred_element_type=jnp.float32,
    )
    spectra = result.reshape(filtered.shape[0], filtered.shape[1], 2 * chan_count)
    rounded = spectra.astype(jnp.bfloat16).reshape(inputs_dev, spec_dev, 2, chan_count)
    ordered = jnp.transpose(rounded, (3, 2, 1, 0))
    turned = lax.all_to_all(ordered, "col", split_axis=0, concat_axis=3, tiled=True)
    across = lax.all_gather(turned, "vert", axis=3, tiled=True)
    row_size = turned.shape[3]
    total_inputs = across.shape[3]
    col_size = total_inputs // lax.axis_size("ta")
    spectra_total = spec_dev * lax.axis_size("ta")
    row_start = lax.axis_index("vert") * row_size
    col_start = lax.axis_index("ta") * col_size
    piece = lax.all_gather(across, "ta", axis=2, tiled=True)
    rows = lax.dynamic_slice_in_dim(piece, row_start, row_size, 3)
    cols = lax.dynamic_slice_in_dim(piece, col_start, col_size, 3)
    summed = correlate(rows, cols)
    return (summed * (1.0 / spectra_total)).astype(jnp.bfloat16)


def solution(mesh):
    placed = (P(("vert", "col"), "ta"), P(), P())
    return jax.shard_map(
        shards, mesh=mesh, in_specs=placed, out_specs=P("col", None, "vert", "ta"), check_vma=False
    )
```

profile of v0, /device:TPU:7, one launch (start us, length us, event | category | flops | bytes accessed | tf_op | source)
XLA Modules:
  0.0 269.1 jit_solution(4580121909371600414)
XLA Ops:
  6.5 0.0 all-gather.2.cloned.1.call-start
  6.5 7.5 %copy.46 = bf16[8,4,8,16384]{3,2,0,1:T(8,128)(2,1)} copy(bf16[8,4,8,16384]{3,2,1,0:T(8,128)(2,1)} %bitcast.47) | data formatting | bytes 16777216 | tf_op jit(solution)/shard_map/reshape | solution.py:42
  14.0 0.0 copy-start
  14.0 0.0 copy-start.1
  14.0 3.2 %slice.40 = bf16[64,3,16384]{2,0,1:T(8,128)(2,1)S(1)} slice(bf16[64,4,16384]{2,0,1:T(8,128)(2,1)} %bitcast.50), slice={[0:64], [1:4], [0:16384]} | slice | bytes 12582912 | tf_op jit(solution)/shard_map/slice | solution.py:44
  17.3 1.3 collective-permute-start
  18.6 0.0 copy-done
  18.6 0.2 fusion.45
  18.8 0.0 copy-done.1
  18.8 4.2 %fusion.40 = (f32[16384,16]{0,1:T(8,128)S(1)}, f32[16384,16]{0,1:T(8,128)S(1)}) fusion(s32[16]{0:T(128)S(1)} %copy-done.1), kind=kLoop, calls=%fused_computation.43 | loop fusion | flops 3932160 | bytes 2097216 | tf_op jit(solution)/shard_map/cos | solution.py:20
  23.0 132.6 %collective-permute-done = bf16[64,3,16384]{2,0,1:T(8,128)(2,1)S(1)} collective-permute-done((bf16[64,3,16384]{2,0,1:T(8,128)(2,1)S(1)}, bf16[64,3,16384]{2,0,1:T(8,128)(2,1)S(1)}, u32[]{:S(2)}, u32[]{:S(2)}) %collective-permute-start) | collective-permute-done | bytes 6291488 | tf_op jit(solution)/shard_map/ppermute | solution.py:12
  155.6 3.1 %constant_dynamic-update-slice_fusion.1 = bf16[64,7,16384]{2,0,1:T(8,128)(2,1)} fusion(bf16[64,3,16384]{2,0,1:T(8,128)(2,1)S(1)} %collective-permute-done), kind=kLoop, calls=%fused_computation.49 | loop fusion | bytes 12582912
  158.6 7.6 %constant_dynamic-update-slice_fusion = bf16[64,7,16384]{2,0,1:T(8,128)(2,1)} fusion(bf16[64,7,16384]{2,0,1:T(8,128)(2,1)} %constant_dynamic-update-slice_fusion.1, bf16[8,4,8,16384]{3,2,1,0:T(8,128)(2,1)} %bitcast.48), kind=kLoop, calls=%fused_computation.48 | loop fusion | bytes 16777216 | tf_op jit(solution)/shard_map/concatenate | solution.py:45
  166.2 31.6 %fusion.23 = bf16[64,4,32]{0,2,1:T(8,128)(2,1)S(1)} fusion(f32[16384,16]{0,1:T(8,128)S(1)} %get-tuple-element.12, f32[16384,16]{0,1:T(8,128)S(1)} %get-tuple-element.11, bf16[64,7,16384]{2,0,1:T(8,128)(2,1)} %constant_dynamic-update-slice_fusion, f32[16384]{0:T(1024)S(1)} %bitcast.59, f32[16384]{0:T(1024)S(1)} %bitcast.60, f32[16384]{0:T(1024)S(1)} %bitcast.58, ...), kind=kOutput, calls=%fused_computation.29 | convolution fusion | flops 1657806848 | bytes 35930112 | tf_op jit(solution)/shard_map/dot_general | solution.py:51
  197.9 0.1 reshape.31
  198.0 14.6 %all_to_all.18 = bf16[4,2,1024]{2,1,0:T(2,128)(2,1)S(1)} all-to-all(bf16[4,2,1024]{2,1,0:T(2,128)(2,1)S(1)} %reshape.31), channel_id=1, replica_groups=mesh['ta'=4,'col'=4,'vert'=16] {'col'}, dimensions={0} | all-to-all | bytes 32768 | tf_op jit(solution)/shard_map/all_to_all | solution.py:60
  212.6 0.1 reshape.32
  212.7 0.1 all_to_all.16
  212.8 24.6 %all_gather.6 = bf16[4,2,4,4096]{3,0,1,2:T(4,128)(2,1)} all-gather(bf16[4,2,4,256]{3,0,1,2:T(4,128)(2,1)S(1)} %all_to_all.16), channel_id=1, replica_groups=mesh['ta'=4,'col'=4,'vert'=16] {'vert'}, dimensions={3}, use_global_device_ids=true | all-gather | bytes 278528 | tf_op jit(solution)/shard_map/all_gather | solution.py:61
  237.4 0.0 all-gather.2.cloned.1.call-update
  237.5 17.8 %all-gather.2.cloned.1.call-done = bf16[4,2,16,4096]{3,0,1,2:T(4,128)(2,1)} async-done(((bf16[4,2,4,4096]{3,0,1,2:T(4,128)(2,1)}), bf16[4,2,16,4096]{3,0,1,2:T(4,128)(2,1)}) %all-gather.2.cloned.1.call-update) | async-done | bytes 1048592 | tf_op jit(solution)/shard_map/all_gather | solution.py:68
  255.2 1.0 constant_dynamic-slice_fusion.2
  256.3 0.2 copy.23
  256.5 0.9 constant_dynamic-slice_fusion.3
  257.4 1.1 constant_dynamic-slice_fusion.1
  258.4 0.1 copy_bitcast_fusion.1
  258.5 1.3 multiply_convert_fusion
  259.8 2.5 copy.47
  (3 shorter events, 0.1 us)
Async XLA Ops:
  6.5 248.7 %all-gather.2.cloned.1.call-start = ((), (), s32[]{:S(2)}) async-start(), calls=%async_computation.1 | async-start | bytes 1310720 | tf_op jit(solution)/shard_map/all_gather | solution.py:68
  14.0 4.6 %copy-start = (f32[4,16384]{1,0:T(4,128)S(1)}, f32[4,16384]{1,0:T(4,128)}, u32[]{:S(2)}) copy-start(f32[4,16384]{1,0:T(4,128)} %param.4) | copy-start | bytes 786436
  14.0 4.8 %copy-start.1 = (s32[16]{0:T(128)S(1)}, s32[16]{0:T(128)}, u32[]{:S(2)}) copy-start(s32[16]{0:T(128)} %param.5) | copy-start | bytes 196
  17.3 138.3 %collective-permute-start = (bf16[64,3,16384]{2,0,1:T(8,128)(2,1)S(1)}, bf16[64,3,16384]{2,0,1:T(8,128)(2,1)S(1)}, u32[]{:S(2)}, u32[]{:S(2)}) collective-permute-start(bf16[64,3,16384]{2,0,1:T(8,128)(2,1)S(1)} %slice.40), channel_id=1, source_target_pairs={{0,64},{64,128},{128,192},{1,65},{65,129},{129,193},{2,66},{66,130... | collective-permute-start | bytes 18874376 | tf_op jit(solution)/shard_map/ppermute | solution.py:12
Sparse Core Ops, SparseCore 0:
  237.6 17.5 all-gather.1
where the time goes:
time: 271 us; the launch traced here: 269 us
  waiting for transfers between devices  150 us (55%)
  blocking collectives  39.3 us (15%)
  matrix products  32.9 us (12%)
  local copies, waits for them, and re-layouts  27.5 us (10%)
  between operations  13.5 us (5%)
  other arithmetic  4.27 us (2%)
    ppermute x1, waiting for transfers between devices, passed_along(): return lax.ppermute(shard, axis, pairs)  133 us
    dot_general x1, matrix products, shards(): jnp.dot(filtered.reshape(-1, frame_len), table, precision=lax.Precision.H...  31.6 us
    all_gather x1, blocking collectives, shards(): across = lax.all_gather(turned, 'vert', axis=3, tiled=True)  24.6 us
    all_gather x1, waiting for transfers between devices, shards(): piece = lax.all_gather(across, 'ta', axis=2, tiled=True)  17.8 us
    all_to_all x1, blocking collectives, shards(): lax.all_to_all(ordered, 'col', split_axis=0, concat_axis=3, tiled=True)  14.6 us
    concatenate x1, local copies, waits for them, and re-layouts, shards(): extended = jnp.concatenate([previous, frames], axis=1)  7.58 us
    reshape x1, local copies, waits for them, and re-layouts, shards(): frames = voltages.reshape(inputs_dev, spec_dev, frame_len)  7.48 us
  transfers between devices with their start and end apart: 2, of which 2 were waited for; matrix products, arithmetic and copies ran while one was open for 2% of the time, Pallas kernels for 0%

commit v1 on v0

v1 whole, which is shorter than its diff:
```python
import functools
import math

import jax
import jax.numpy as jnp
from jax import lax
from jax.experimental import pallas as pl
from jax.experimental.pallas import tpu as pltpu
from jax.sharding import Mesh, PartitionSpec as P

FRAMES = 4
TAPS = 4
CHUNK = 2048
LANES = 128
ROWS = 32
HALF = 64


def row_channels(chan_ref, shape):
    row = lax.broadcasted_iota(jnp.int32, shape, 0)
    which = row // 8 * 4 + row % 4
    chan = jnp.zeros(shape, jnp.int32)
    for c in range(16):
        chan = jnp.where(which == c, chan_ref[c], chan)
    return chan, row // 4 % 2


def filterbank_kernel(chan_ref, v0, v1, v2, v3, taps_ref, own_ref, next_ref, cos_ref, sin_ref, chan_tab, acc_ref):
    step = pl.program_id(0)
    length = pl.num_programs(0) * CHUNK
    turn = 2.0 * math.pi / length
    mask = length - 1

    @pl.when(step == 0)
    def _():
        chan, _ = row_channels(chan_ref, (ROWS, LANES))
        chan_tab[...] = chan
        lane = lax.broadcasted_iota(jnp.int32, (ROWS, LANES), 1)
        fine = ((lane * chan) & mask).astype(jnp.float32) * turn
        fine_cos, fine_sin = jnp.cos(fine), jnp.sin(fine)
        coarse = ((lane * LANES * chan) & mask).astype(jnp.float32) * turn
        coarse_cos, coarse_sin = jnp.cos(coarse), jnp.sin(coarse)
        for u in range(CHUNK // LANES):
            at = slice(u * LANES, (u + 1) * LANES)
            cu, su = coarse_cos[:, u : u + 1], coarse_sin[:, u : u + 1]
            cos_ref[:, at] = cu * fine_cos - su * fine_sin
            sin_ref[:, at] = su * fine_cos + cu * fine_sin

    part = lax.broadcasted_iota(jnp.int32, (ROWS, LANES), 0) // 4 % 2
    base = ((chan_tab[...] * (step * CHUNK) + part * (length // 4)) & mask).astype(jnp.float32) * turn
    scale = 1.0 / math.sqrt(length)
    base_cos = (jnp.cos(base) * scale)[:, :1]
    base_sin = (jnp.sin(base) * scale)[:, :1]
    table = base_cos * cos_ref[...] - base_sin * sin_ref[...]
    high, low = [], []
    for t in range(TAPS):
        w = table * taps_ref[t : t + 1, :]
        h = w.astype(jnp.bfloat16)
        high.append(h)
        low.append((w - h.astype(jnp.float32)).astype(jnp.bfloat16))
    weights = jnp.concatenate(high + low, axis=0)
    frames = jnp.concatenate([v0[...], v1[...], v2[...], v3[...]], axis=0)
    prod = lax.dot_general(
        weights, frames, (((1,), (1,)), ((), ())), preferred_element_type=jnp.float32
    )
    acc_ref[...] = jnp.where(step == 0, 0.0, acc_ref[...]) + prod

    @pl.when(step == pl.num_programs(0) - 1)
    def _():
        g = acc_ref[: TAPS * ROWS] + acc_ref[TAPS * ROWS :]

        def term(t, f):
            return g[t * ROWS : (t + 1) * ROWS, f * HALF : (f + 1) * HALF]

        own, after = [], []
        for s in range(FRAMES):
            own.append(sum(term(f - s + 3, f) for f in range(s + 1)))
            if s < TAPS - 1:
                after.append(sum(term(f - 1 - s, f) for f in range(s + 1, FRAMES)))
        after.append(jnp.zeros_like(after[0]))
        own_ref[...] = jnp.concatenate(own, axis=1)
        next_ref[...] = jnp.concatenate(after, axis=1)


def filterbank(voltages, taps, channels):
    frame_len = taps.shape[1]
    steps = frame_len // CHUNK

    def frame(f):
        return pl.BlockSpec((HALF, CHUNK), lambda j, f=f: (0, f * steps + j))

    whole = pl.BlockSpec((ROWS, FRAMES * HALF), lambda j: (0, 0))
    out = jax.ShapeDtypeStruct((ROWS, FRAMES * HALF), jnp.float32)
    return pl.pallas_call(
        filterbank_kernel,
        grid=(steps,),
        in_specs=[pl.BlockSpec(memory_space=pltpu.SMEM)]
        + [frame(f) for f in range(FRAMES)]
        + [pl.BlockSpec((TAPS, CHUNK), lambda j: (0, j))],
        out_specs=[whole, whole],
        out_shape=[out, out],
        scratch_shapes=[
            pltpu.VMEM((ROWS, CHUNK), jnp.float32),
            pltpu.VMEM((ROWS, CHUNK), jnp.float32),
            pltpu.VMEM((ROWS, LANES), jnp.int32),
            pltpu.VMEM((2 * TAPS * ROWS, FRAMES * HALF), jnp.float32),
        ],
        compiler_params=pltpu.CompilerParams(vmem_limit_bytes=24 * 2**20),
        name="filterbank",
    )(channels, voltages, voltages, voltages, voltages, taps)


def combine_kernel(own_ref, before_ref, out_ref):
    total = own_ref[...] + before_ref[...]
    for c in range(4):
        rows = total[c * 8 : (c + 1) * 8]
        piece = jnp.concatenate([rows[:, :LANES], rows[:, LANES:]], axis=0).astype(jnp.bfloat16)
        for x in range(4):
            for y in range(4):
                out_ref[(x * 4 + c) * 4 + y] = piece


def combine(own, before):
    return pl.pallas_call(
        combine_kernel,
        out_shape=jax.ShapeDtypeStruct((64, 16, LANES), jnp.bfloat16),
        name="combine",
    )(own, before)


def arrange_kernel(got_ref, left_ref, right_ref):
    low = lax.broadcasted_iota(jnp.int32, (16, LANES), 1) < HALF

    def gathered(y):
        blocks = []
        for x in range(4):
            first, second = [], []
            for pair in range(2):
                even = got_ref[(x * 4 + 2 * pair) * 4 + y].astype(jnp.float32)
                odd = got_ref[(x * 4 + 2 * pair + 1) * 4 + y].astype(jnp.float32)
                first.append(jnp.where(low, even, pltpu.roll(odd, HALF, 1)))
                second.append(jnp.where(low, pltpu.roll(even, HALF, 1), odd))
            blocks += [jnp.concatenate(first, axis=1), jnp.concatenate(second, axis=1)]
        return jnp.concatenate(blocks, axis=0)

    right_ref[...] = gathered(lax.axis_index("x")).astype(jnp.bfloat16)
    left = gathered(lax.axis_index("y"))
    turned = []
    for g in range(16):
        rows = left[g * 8 : (g + 1) * 8]
        turned.append(pltpu.roll(rows, 4, 0))
    turned = jnp.concatenate(turned, axis=0)
    depth = lax.broadcasted_iota(jnp.int32, turned.shape, 0)
    turned = jnp.where(depth // 4 % 2 == 0, turned, -turned)
    lane = lax.broadcasted_iota(jnp.int32, (256, LANES), 1)
    for part, values in enumerate((left, turned)):
        flipped = values.T
        for c in range(4):
            left_ref[c, part] = jnp.where(lane % 4 == c, flipped, 0.0).astype(jnp.bfloat16)


def arrange(got):
    return pl.pallas_call(
        arrange_kernel,
        out_shape=[
            jax.ShapeDtypeStruct((4, 2, 256, LANES), jnp.bfloat16),
            jax.ShapeDtypeStruct((LANES, 256), jnp.bfloat16),
        ],
        name="arrange",
    )(got)


def correlate_kernel(scale, left_ref, right_ref, out_ref):
    right = right_ref[0]
    for c in range(4):
        for part in range(2):
            product = jnp.dot(left_ref[c, part], right, preferred_element_type=jnp.float32)
            out_ref[c, part] = (product * scale).astype(jnp.bfloat16)


def correlate(left, right, scale):
    return pl.pallas_call(
        functools.partial(correlate_kernel, scale),
        grid=(4,),
        in_specs=[
            pl.BlockSpec((4, 2, 256, LANES), lambda q: (0, 0, 0, 0)),
            pl.BlockSpec((1, LANES, 256), lambda q: (q, 0, 0)),
        ],
        out_specs=pl.BlockSpec((4, 2, 256, 256), lambda q: (0, 0, 0, q)),
        out_shape=jax.ShapeDtypeStruct((4, 2, 256, 1024), jnp.bfloat16),
        name="correlate",
    )(left, right)


def shards(voltages, taps, channels):
    own, after = filterbank(voltages, taps, channels)
    before = lax.ppermute(after, "x", [(i, i + 1) for i in range(3)])
    pieces = combine(own, before)
    got = lax.all_to_all(pieces, ("x", "zh", "y"), 0, 0, tiled=True)
    left, quarter = arrange(got)
    right = lax.all_gather(quarter, ("zl", "co"), axis=0)
    return correlate(left, right, 1.0 / 16.0)


def solution(mesh):
    fine = Mesh(mesh.devices.reshape(4, 4, 4, 2, 2), ("x", "zh", "y", "zl", "co"))
    placed = (P(("y", "zl", "co", "zh"), "x"), P(), P())
    return jax.shard_map(
        shards,
        mesh=fine,
        in_specs=placed,
        out_specs=P("zh", None, ("y", "zl", "co"), "x"),
        check_vma=False,
    )
```

time: 271 us -> 64.2 us (0.24)
  the two profiles are of different devices: /device:TPU:7 before, /device:TPU:1 now
where the time goes in v1:
time: 64.2 us; the launch traced here: 63.7 us
  blocking collectives  37.9 us (59%)
  Pallas kernels  14.6 us (23%)
  local copies, waits for them, and re-layouts  6.18 us (10%)
  starting transfers between devices  3.93 us (6%)
  waiting for transfers between devices  1 us (2%)
    all_to_all x1, blocking collectives, shards(): got = lax.all_to_all(pieces, ('x', 'zh', 'y'), 0, 0, tiled=True)  27.5 us
    all_gather x1, blocking collectives, shards(): right = lax.all_gather(quarter, ('zl', 'co'), axis=0)  10.4 us
    pallas_call x1, Pallas kernels, filterbank(): pl.pallas_call(filterbank_kernel, grid=(steps,), in_specs=[pl.BlockSpec(m...  6.48 us
    unnamed x10, local copies, waits for them, and re-layouts  6.18 us
    pallas_call x1, Pallas kernels, correlate(): pl.pallas_call(functools.partial(correlate_kernel, scale), grid=(4,), in_...  4.7 us
    ppermute x1, starting transfers between devices, shards(): before = lax.ppermute(after, 'x', [(i, i + 1) for i in range(3)])  3.93 us
    pallas_call x1, Pallas kernels, arrange(): pl.pallas_call(arrange_kernel, out_shape=[jax.ShapeDtypeStruct((4, 2, 256...  1.98 us
    pallas_call x1, Pallas kernels, combine(): pl.pallas_call(combine_kernel, out_shape=jax.ShapeDtypeStruct((64, 16, LA...  1.5 us
  transfers between devices with their start and end apart: 1, of which 1 were waited for; matrix products, arithmetic and copies ran while one was open for 0% of the time, Pallas kernels for 0%

profile of v1, /device:TPU:1, one launch (start us, length us, event | category | flops | bytes accessed | tf_op | source)
XLA Modules:
  0.0 63.7 jit_solution(10417679953226030264)
XLA Ops:
  0.0 0.0 copy-start
  0.0 3.4 %copy-done = bf16[64,65536]{1,0:T(8,128)(2,1)S(1)} copy-done((bf16[64,65536]{1,0:T(8,128)(2,1)S(1)}, bf16[64,65536]{1,0:T(8,128)(2,1)}, u32[]{:S(2)}) %copy-start) | copy-done | bytes 8388632
  3.4 0.0 copy-start.1
  3.4 0.9 %copy-done.1 = f32[4,16384]{1,0:T(4,128)S(1)} copy-done((f32[4,16384]{1,0:T(4,128)S(1)}, f32[4,16384]{1,0:T(4,128)}, u32[]{:S(2)}) %copy-start.1) | copy-done | bytes 262168
  4.3 0.0 copy-start.3
  4.3 0.7 %copy-done.3 = s32[16]{0:T(128)S(1)} copy-done((s32[16]{0:T(128)S(1)}, s32[16]{0:T(128)}, u32[]{:S(2)}) %copy-start.3) | copy-done | bytes 88
  5.0 6.5 %filterbank.1 = (f32[32,256]{1,0:T(8,128)S(1)}, f32[32,256]{1,0:T(8,128)S(1)}) custom-call(s32[16]{0:T(128)S(1)} %copy-done.3, bf16[64,65536]{1,0:T(8,128)(2,1)S(1)} %copy-done, bf16[64,65536]{1,0:T(8,128)(2,1)S(1)} %copy-done, bf16[64,65536]{1,0:T(8,128)(2,1)S(1)} %copy-done, bf16[64,65536]{1,0:T(8,128)(2,1)S(1)} %copy-done, f32[4,16384]{1,0:T(4,128)S(1)} %copy-done.1), custom_call_target="tpu_custom_call" | custom-call | tf_op jit(solution)/shard_map/filterbank/pallas_call | solution.py:94
  11.5 0.0 copy-start.2
  11.5 0.6 copy-done.2
  12.1 3.9 %collective-permute-start = (f32[32,256]{1,0:T(8,128)S(1)}, f32[32,256]{1,0:T(8,128)S(1)}, u32[]{:S(2)}, u32[]{:S(2)}) collective-permute-start(f32[32,256]{1,0:T(8,128)S(1)} %get-tuple-element.10), channel_id=1, source_target_pairs={{0,64},{64,128},{128,192},{1,65},{65,129},{129,193},{2,66},{66,130... | collective-permute-start | bytes 98312 | tf_op jit(solution)/shard_map/ppermute | solution.py:197
  16.0 1.0 %collective-permute-done.before_ref = f32[32,256]{1,0:T(8,128)S(1)} collective-permute-done((f32[32,256]{1,0:T(8,128)S(1)}, f32[32,256]{1,0:T(8,128)S(1)}, u32[]{:S(2)}, u32[]{:S(2)}) %collective-permute-start) | collective-permute-done | bytes 32800 | tf_op jit(solution)/shard_map/ppermute | solution.py:197
  17.0 0.0 copy-start.4
  17.0 0.6 copy-done.4
  17.6 1.5 %combine.1 = bf16[64,16,128]{2,1,0:T(8,128)(2,1)} custom-call(f32[32,256]{1,0:T(8,128)} %copy-done.2, f32[32,256]{1,0:T(8,128)} %copy-done.4), custom_call_target="tpu_custom_call" | custom-call | tf_op jit(solution)/shard_map/combine/pallas_call | solution.py:124
  19.1 27.5 %all_to_all.5.got_ref = bf16[64,16,128]{2,1,0:T(8,128)(2,1)} all-to-all(bf16[64,16,128]{2,1,0:T(8,128)(2,1)} %combine.1), channel_id=1, replica_groups=mesh['x'=4,'zh'=4,'y'=4,'zl'=2,'co'=2] {'x','zh','y'}, dimensions={0} | all-to-all | bytes 524288 | tf_op jit(solution)/shard_map/all_to_all | solution.py:199
  46.7 2.0 %arrange.1 = (bf16[4,2,256,128]{3,2,1,0:T(8,128)(2,1)}, bf16[128,256]{1,0:T(8,128)(2,1)}) custom-call(bf16[64,16,128]{2,1,0:T(8,128)(2,1)} %all_to_all.5.got_ref), custom_call_target="tpu_custom_call" | custom-call | tf_op jit(solution)/shard_map/arrange/pallas_call | solution.py:163
  48.6 10.4 %all-gather = bf16[512,256]{1,0:T(8,128)(2,1)} all-gather(bf16[128,256]{1,0:T(8,128)(2,1)} %get-tuple-element.12), channel_id=2, replica_groups=mesh['x'=4,'zh'=4,'y'=4,'zl'=2,'co'=2] {'zl','co'}, dimensions={0}, use_global_device_ids=true | all-gather | bytes 327680 | tf_op jit(solution)/shard_map/all_gather | solution.py:201
  59.0 4.7 %correlate.1 = bf16[4,2,256,1024]{3,2,1,0:T(8,128)(2,1)} custom-call(bf16[4,2,256,128]{3,2,1,0:T(8,128)(2,1)} %get-tuple-element.11.left_ref, bf16[4,128,256]{2,1,0:T(8,128)(2,1)} %bitcast.1), custom_call_target="tpu_custom_call" | custom-call | tf_op jit(solution)/shard_map/correlate/pallas_call | solution.py:182
Async XLA Ops:
  0.0 3.4 %copy-start = (bf16[64,65536]{1,0:T(8,128)(2,1)S(1)}, bf16[64,65536]{1,0:T(8,128)(2,1)}, u32[]{:S(2)}) copy-start(bf16[64,65536]{1,0:T(8,128)(2,1)} %v3.1) | copy-start | bytes 25165828
  3.4 0.9 %copy-start.1 = (f32[4,16384]{1,0:T(4,128)S(1)}, f32[4,16384]{1,0:T(4,128)}, u32[]{:S(2)}) copy-start(f32[4,16384]{1,0:T(4,128)} %taps_ref.1) | copy-start | bytes 786436
  4.3 0.7 %copy-start.3 = (s32[16]{0:T(128)S(1)}, s32[16]{0:T(128)}, u32[]{:S(2)}) copy-start(s32[16]{0:T(128)} %chan_ref.1) | copy-start | bytes 196
  11.5 0.6 copy-start.2
  12.1 4.9 %collective-permute-start = (f32[32,256]{1,0:T(8,128)S(1)}, f32[32,256]{1,0:T(8,128)S(1)}, u32[]{:S(2)}, u32[]{:S(2)}) collective-permute-start(f32[32,256]{1,0:T(8,128)S(1)} %get-tuple-element.10), channel_id=1, source_target_pairs={{0,64},{64,128},{128,192},{1,65},{65,129},{129,193},{2,66},{66,130... | collective-permute-start | bytes 98312 | tf_op jit(solution)/shard_map/ppermute | solution.py:197
  17.0 0.6 copy-start.4

commit v2 on v0

v2 whole, which is shorter than its diff:
```python
import functools
import math

import jax
import jax.numpy as jnp
from jax import lax
from jax.experimental import pallas as pl
from jax.experimental.pallas import tpu as pltpu
from jax.sharding import Mesh, PartitionSpec as P

FRAMES = 4
TAPS = 4
CHUNK = 4096
LANES = 128
ROWS = 32
HALF = 64
VMEM_LIMIT = 60 * 2**20
ARR_LIMIT = 16 * 2**20
CORR_LIMIT = 16 * 2**20


AXES = ("x", "zh", "y", "zl", "co")


def first_z():
    return 2 * lax.axis_index("zl") + lax.axis_index("co")


def first_x():
    return lax.axis_index("y")


def exchange_groups():
    groups = []
    for y in range(4):
        for zl in range(2):
            for co in range(2):
                members = [((p + y) % 4, (q + 2 * zl + co) % 4) for q in range(4) for p in range(4)]
                groups.append([(((x * 4 + z) * 4 + y) * 2 + zl) * 2 + co for x, z in members])
    return groups


def row_channels(chan_ref, shape):
    row = lax.broadcasted_iota(jnp.int32, shape, 0)
    which = row // 8 * 4 + row % 4
    chan = jnp.zeros(shape, jnp.int32)
    for c in range(16):
        chan = jnp.where(which == c, chan_ref[c], chan)
    return chan, row // 4 % 2


def filterbank_kernel(chan_ref, volt_ref, taps_ref, out_ref, frames_ref, coef_ref, cos_ref, sin_ref, base_ref, acc_ref, volt_sem, coef_sem):
    length = taps_ref.shape[1]
    steps = length // CHUNK
    turn = 2.0 * math.pi / length
    mask = length - 1

    def volt_copy(j, f):
        return pltpu.make_async_copy(
            volt_ref.at[:, pl.ds(pl.multiple_of(f * length + j * CHUNK, CHUNK), CHUNK)],
            frames_ref.at[j, pl.ds(f * HALF, HALF)],
            volt_sem.at[j, f],
        )

    def taps_copy(j):
        at = pl.ds(pl.multiple_of(j * CHUNK, CHUNK), CHUNK)
        return pltpu.make_async_copy(taps_ref.at[:, at], coef_ref.at[j], coef_sem.at[j])

    @pl.loop(0, steps)
    def _(j):
        for f in range(FRAMES):
            volt_copy(j, f).start()
        taps_copy(j).start()

    chan, part = row_channels(chan_ref, (ROWS, LANES))
    lane = lax.broadcasted_iota(jnp.int32, (ROWS, LANES), 1)

    def angles(index, shift):
        phase = ((index * chan + shift) & mask).astype(jnp.float32) * turn
        return jnp.cos(phase), jnp.sin(phase)

    fine_cos, fine_sin = angles(lane, 0)
    coarse_cos, coarse_sin = angles(lane * LANES, 0)
    for u in range(CHUNK // LANES):
        at = slice(u * LANES, (u + 1) * LANES)
        cu, su = coarse_cos[:, u : u + 1], coarse_sin[:, u : u + 1]
        cos_ref[:, at] = cu * fine_cos - su * fine_sin
        sin_ref[:, at] = su * fine_cos + cu * fine_sin
    base_cos, base_sin = angles(lane * CHUNK, part * (length // 4))
    scale = 1.0 / math.sqrt(length)
    base_cos, base_sin = base_cos * scale, base_sin * scale

    for j in range(steps):
        base_ref[j] = jnp.broadcast_to(base_cos[:, j : j + 1], (ROWS, LANES))
        base_ref[steps + j] = jnp.broadcast_to(base_sin[:, j : j + 1], (ROWS, LANES))
    acc_ref[...] = jnp.zeros_like(acc_ref)

    def chunk(j, carry):
        taps_copy(j).wait()
        for f in range(FRAMES):
            volt_copy(j, f).wait()
        turn_cos, turn_sin = base_ref[j], base_ref[steps + j]
        high, low = [], []
        for u in range(CHUNK // LANES):
            at = slice(u * LANES, (u + 1) * LANES)
            table = turn_cos * cos_ref[:, at] - turn_sin * sin_ref[:, at]
            w = jnp.concatenate([table * coef_ref[j, t : t + 1, at] for t in range(TAPS)], axis=0)
            h = w.astype(jnp.bfloat16)
            high.append(h)
            low.append((w - h.astype(jnp.float32)).astype(jnp.bfloat16))
        weights = jnp.concatenate(
            [jnp.concatenate(high, axis=1), jnp.concatenate(low, axis=1)], axis=0
        )
        acc_ref[...] = acc_ref[...] + lax.dot_general(
            weights, frames_ref[j], (((1,), (1,)), ((), ())), preferred_element_type=jnp.float32
        )
        return carry

    lax.fori_loop(0, steps, chunk, 0)
    g = acc_ref[: TAPS * ROWS] + acc_ref[TAPS * ROWS :]

    def term(t, f):
        return g[t * ROWS : (t + 1) * ROWS, f * HALF : (f + 1) * HALF]

    own, after = [], []
    for s in range(FRAMES):
        own.append(sum(term(f - s + 3, f) for f in range(s + 1)))
        if s < TAPS - 1:
            after.append(sum(term(f - 1 - s, f) for f in range(s + 1, FRAMES)))
    after.append(jnp.zeros_like(after[0]))
    own = jnp.concatenate(own, axis=1)
    after = jnp.concatenate(after, axis=1)
    for c in range(4):
        rows = slice(c * 8, (c + 1) * 8)
        piece = [part[rows, at : at + LANES] for part in (own, after) for at in (0, LANES)]
        piece = jnp.concatenate(piece, axis=0)
        place = (c - first_z()) % 4
        for x in range(4):
            out_ref[place * 4 + x] = piece


def filterbank(voltages, taps, channels):
    steps = taps.shape[1] // CHUNK
    return pl.pallas_call(
        filterbank_kernel,
        in_specs=[
            pl.BlockSpec(memory_space=pltpu.SMEM),
            pl.BlockSpec(memory_space=pl.ANY),
            pl.BlockSpec(memory_space=pl.ANY),
        ],
        out_shape=jax.ShapeDtypeStruct((16, 32, LANES), jnp.float32),
        scratch_shapes=[
            pltpu.VMEM((steps, FRAMES * HALF, CHUNK), jnp.bfloat16),
            pltpu.VMEM((steps, TAPS, CHUNK), jnp.float32),
            pltpu.VMEM((ROWS, CHUNK), jnp.float32),
            pltpu.VMEM((ROWS, CHUNK), jnp.float32),
            pltpu.VMEM((2 * steps, ROWS, LANES), jnp.float32),
            pltpu.VMEM((2 * TAPS * ROWS, FRAMES * HALF), jnp.float32),
            pltpu.SemaphoreType.DMA((steps, FRAMES)),
            pltpu.SemaphoreType.DMA((steps,)),
        ],
        compiler_params=pltpu.CompilerParams(vmem_limit_bytes=VMEM_LIMIT),
        name="filterbank",
    )(channels, voltages, taps)


def arrange_kernel(got_ref, rows_ref):
    low = lax.broadcasted_iota(jnp.int32, (8, LANES), 1) < HALF

    turn_x, turn_z = first_x(), first_z()

    def spectra(x, col, late):
        def part(x, at):
            place = (col - turn_z) % 4 * 4 + (x - turn_x) % 4
            return got_ref[place, pl.ds(at, 8)]

        total = part(x, 8 * late)
        if x > 0:
            total = total + part(x - 1, 16 + 8 * late)
        return total.astype(jnp.bfloat16).astype(jnp.float32)

    for x in range(4):
        first, second = [], []
        for late in range(2):
            a, b = [], []
            for pair in range(2):
                even = spectra(x, 2 * pair, late)
                odd = spectra(x, 2 * pair + 1, late)
                a.append(jnp.where(low, even, pltpu.roll(odd, HALF, 1)))
                b.append(jnp.where(low, pltpu.roll(even, HALF, 1), odd))
            first.append(jnp.concatenate(a, axis=1))
            second.append(jnp.concatenate(b, axis=1))
        block = jnp.concatenate(first + second, axis=0)
        rows_ref[32 * x : 32 * (x + 1)] = block.astype(jnp.bfloat16)


def arrange(got):
    return pl.pallas_call(
        arrange_kernel,
        out_shape=jax.ShapeDtypeStruct((LANES, 256), jnp.bfloat16),
        compiler_params=pltpu.CompilerParams(vmem_limit_bytes=ARR_LIMIT),
        name="arrange",
    )(got)


def correlate_kernel(scale, rows_ref, near_ref, near_other_ref, far_ref, far_other_ref, out_ref, left_ref, right_ref, held_ref, sem):
    left = rows_ref[...].astype(jnp.float32)
    turned = [pltpu.roll(left[g * 8 : (g + 1) * 8], 4, 0) for g in range(LANES // 8)]
    turned = jnp.concatenate(turned, axis=0)
    depth = lax.broadcasted_iota(jnp.int32, turned.shape, 0)
    turned = jnp.where(depth // 4 % 2 == 0, turned, -turned)
    left_ref[0] = left.T
    left_ref[1] = turned.T
    width = near_ref.shape[1]
    mine = 2 * lax.axis_index("zl") + lax.axis_index("co")
    for k, block in enumerate((near_ref, near_other_ref, far_ref, far_other_ref)):
        for place in range(4):
            @pl.when(mine == place ^ k)
            def _():
                right_ref[:, place * width : (place + 1) * width] = block[...]

    lane = lax.broadcasted_iota(jnp.int32, left_ref.shape[1:], 1)

    def copy(k):
        return pltpu.make_async_copy(held_ref.at[k], out_ref.at[k // 2, k % 2], sem.at[k])

    @pl.loop(0, 8)
    def _(k):
        chosen = jnp.where(lane % 4 == k // 2, left_ref[k % 2], 0.0).astype(jnp.bfloat16)
        product = jnp.dot(chosen, right_ref[...], preferred_element_type=jnp.float32)
        held_ref[k] = (product * scale).astype(jnp.bfloat16)
        copy(k).start()

    @pl.loop(0, 8)
    def _(k):
        copy(k).wait()


def correlate(rows, blocks, scale):
    depth, width = rows.shape
    return pl.pallas_call(
        functools.partial(correlate_kernel, scale),
        in_specs=[pl.BlockSpec(memory_space=pltpu.VMEM)] * 5,
        out_specs=pl.BlockSpec(memory_space=pl.ANY),
        out_shape=jax.ShapeDtypeStruct((4, 2, width, 4 * width), jnp.bfloat16),
        scratch_shapes=[
            pltpu.VMEM((2, width, depth), jnp.float32),
            pltpu.VMEM((depth, 4 * width), jnp.bfloat16),
            pltpu.VMEM((8, width, 4 * width), jnp.bfloat16),
            pltpu.SemaphoreType.DMA((8,)),
        ],
        compiler_params=pltpu.CompilerParams(vmem_limit_bytes=CORR_LIMIT),
        name="correlate",
    )(rows, *blocks)


def across():
    pairs = []
    for x in range(4):
        for y in range(4):
            source = (x + 2 - (y - x)) % 4
            pairs.append((source * 4 + x, x * 4 + y))
    return pairs


def shards(voltages, taps, channels):
    pieces = filterbank(voltages, taps, channels)
    got = lax.all_to_all(pieces, AXES, 0, 0, axis_index_groups=exchange_groups(), tiled=True)
    rows = arrange(got)
    swap = [(0, 1), (1, 0)]
    pairs = [(2 * s + z, 2 * d + 1 - z) for s, d in across() for z in range(2)]
    near = lax.ppermute(rows, ("x", "y"), across())
    far = lax.ppermute(rows, ("x", "y", "zl"), pairs)
    near_other = lax.ppermute(near, "co", swap)
    far_other = lax.ppermute(far, "co", swap)
    return correlate(rows, (near, near_other, far, far_other), 1.0 / 16.0)


def solution(mesh):
    fine = Mesh(mesh.devices.reshape(4, 4, 4, 2, 2), ("x", "zh", "y", "zl", "co"))
    placed = (P(("y", "zl", "co", "zh"), "x"), P(), P())
    return jax.shard_map(
        shards,
        mesh=fine,
        in_specs=placed,
        out_specs=P("zh", None, ("y", "zl", "co"), "x"),
        check_vma=False,
    )
```

time: 271 us -> 44.5 us (0.16)
  waiting for transfers between devices: 150 us -> 6.51 us
  matrix products: 32.9 us -> 0 us
  local copies, waits for them, and re-layouts: 27.5 us -> 0 us
  blocking collectives: 39.3 us -> 21 us
  between operations: 13.5 us -> 0.02 us
  Pallas kernels: 0 us -> 9.67 us
  starting transfers between devices: 1.29 us -> 7.1 us
  other arithmetic: 4.27 us -> 0 us
    ppermute x1 -> x4, waiting for transfers between devices: 133 us -> 6.51 us  [the longest x1 4.16 us: shards(): far = lax.ppermute(rows, ('x', 'y', 'zl'), pairs)]
    dot_general x2 -> x0, matrix products: 32.9 us -> none  [the longest x1 31.6 us: shards(): jnp.dot(filtered.reshape(-1, frame_len), table, precision=lax.Precision.H...]
    all_gather x1 -> x0, blocking collectives: 24.6 us -> none  [shards(): across = lax.all_gather(turned, 'vert', axis=3, tiled=True)]
    all_gather x1 -> x0, waiting for transfers between devices: 17.8 us -> none  [shards(): piece = lax.all_gather(across, 'ta', axis=2, tiled=True)]
    pallas_call x0 -> x3, Pallas kernels: none -> 9.67 us  [the longest x1 6.23 us: filterbank(): pl.pallas_call(filterbank_kernel, in_specs=[pl.BlockSpec(memory_space=plt...]
    concatenate x1 -> x0, local copies, waits for them, and re-layouts: 7.58 us -> none  [shards(): extended = jnp.concatenate([previous, frames], axis=1)]
    reshape x2 -> x0, local copies, waits for them, and re-layouts: 7.51 us -> none  [the longest x1 7.48 us: shards(): frames = voltages.reshape(inputs_dev, spec_dev, frame_len)]
    all_to_all x1, blocking collectives: 14.6 us -> 21 us  [shards(): lax.all_to_all(pieces, AXES, 0, 0, axis_index_groups=exchange_groups(), t...]
  transfers between devices with their start and end apart: 2 -> 4, of which waited for: 2 -> 3; matrix products, arithmetic and copies ran while one was open for 2% -> 0% of each run, Pallas kernels for 0% -> 0%
where the time goes in v2:
time: 44.5 us; the launch traced here: 44.3 us
  blocking collectives  21 us (47%)
  Pallas kernels  9.67 us (22%)
  starting transfers between devices  7.1 us (16%)
  waiting for transfers between devices  6.51 us (15%)
    all_to_all x1, blocking collectives, shards(): lax.all_to_all(pieces, AXES, 0, 0, axis_index_groups=exchange_groups(), t...  21 us
    pallas_call x1, Pallas kernels, filterbank(): pl.pallas_call(filterbank_kernel, in_specs=[pl.BlockSpec(memory_space=plt...  6.23 us
    ppermute x1, waiting for transfers between devices, shards(): far = lax.ppermute(rows, ('x', 'y', 'zl'), pairs)  4.16 us
    pallas_call x1, Pallas kernels, correlate(): pl.pallas_call(functools.partial(correlate_kernel, scale), in_specs=[pl.B...  3.34 us
    ppermute x1, starting transfers between devices, shards(): far_other = lax.ppermute(far, 'co', swap)  2.74 us
    ppermute x1, starting transfers between devices, shards(): far = lax.ppermute(rows, ('x', 'y', 'zl'), pairs)  1.94 us
    ppermute x1, starting transfers between devices, shards(): near = lax.ppermute(rows, ('x', 'y'), across())  1.93 us
    ppermute x1, waiting for transfers between devices, shards(): near = lax.ppermute(rows, ('x', 'y'), across())  1.44 us
  transfers between devices with their start and end apart: 4, of which 3 were waited for; matrix products, arithmetic and copies ran while one was open for 0% of the time, Pallas kernels for 0%

profile of v2, /device:TPU:7, one launch (start us, length us, event | category | flops | bytes accessed | tf_op | source)
XLA Modules:
  0.0 44.3 jit_solution(6843515415327837766)
XLA Ops:
  0.0 6.2 %filterbank.1 = f32[16,32,128]{2,1,0:T(8,128)} custom-call(s32[16]{0:T(128)} %chan_ref.1, bf16[64,65536]{1,0:T(8,128)(2,1)} %volt_ref.1, f32[4,16384]{1,0:T(4,128)} %taps_ref.1), custom_call_target="tpu_custom_call" | custom-call | tf_op jit(solution)/shard_map/filterbank/pallas_call | solution.py:144
  6.2 21.0 %all_to_all.5.got_ref = f32[16,32,128]{2,1,0:T(8,128)S(1)} all-to-all(f32[16,32,128]{2,1,0:T(8,128)} %filterbank.1), channel_id=1, replica_groups={{0,64,128,192,16,80,144,208,32,96,160,224,48,112,176,240},{17,81,145,20..., dimensions={0} | all-to-all | bytes 524288 | tf_op jit(solution)/shard_map/all_to_all | solution.py:268
  27.2 0.1 arrange.1.rows_ref
  27.3 1.9 %collective-permute-start.2 = (bf16[128,256]{1,0:T(8,128)(2,1)S(1)}, bf16[128,256]{1,0:T(8,128)(2,1)S(1)}, u32[]{:S(2)}, u32[]{:S(2)}) collective-permute-start(bf16[128,256]{1,0:T(8,128)(2,1)S(1)} %arrange.1.rows_ref), channel_id=1, source_target_pairs={{128,2},{130,0},{64,6},{66,4},{0,10},{2,8},{192,14},{194,12},{4,66... | collective-permute-start | bytes 196616 | tf_op jit(solution)/shard_map/ppermute | solution.py:273
  29.3 1.9 %collective-permute-start = (bf16[128,256]{1,0:T(8,128)(2,1)S(1)}, bf16[128,256]{1,0:T(8,128)(2,1)S(1)}, u32[]{:S(2)}, u32[]{:S(2)}) collective-permute-start(bf16[128,256]{1,0:T(8,128)(2,1)S(1)} %arrange.1.rows_ref), channel_id=1, source_target_pairs={{128,0},{64,4},{0,8},{192,12},{4,64},{196,68},{132,72},{68,76},{13... | collective-permute-start | bytes 196616 | tf_op jit(solution)/shard_map/ppermute | solution.py:272
  31.2 4.2 %collective-permute-done.2.far_ref = bf16[128,256]{1,0:T(8,128)(2,1)S(1)} collective-permute-done((bf16[128,256]{1,0:T(8,128)(2,1)S(1)}, bf16[128,256]{1,0:T(8,128)(2,1)S(1)}, u32[]{:S(2)}, u32[]{:S(2)}) %collective-permute-start.2) | collective-permute-done | bytes 65568 | tf_op jit(solution)/shard_map/ppermute | solution.py:273
  35.4 2.7 %collective-permute-start.3 = (bf16[128,256]{1,0:T(8,128)(2,1)S(1)}, bf16[128,256]{1,0:T(8,128)(2,1)S(1)}, u32[]{:S(2)}, u32[]{:S(2)}) collective-permute-start(bf16[128,256]{1,0:T(8,128)(2,1)S(1)} %collective-permute-done.2.far_ref), channel_id=1, source_target_pairs={{0,1},{1,0},{2,3},{3,2},{4,5},{5,4},{6,7},{7,6},{8,9},{9,8},{10,11... | collective-permute-start | bytes 196616 | tf_op jit(solution)/shard_map/ppermute | solution.py:275
  38.1 1.4 %collective-permute-done.near_ref = bf16[128,256]{1,0:T(8,128)(2,1)S(1)} collective-permute-done((bf16[128,256]{1,0:T(8,128)(2,1)S(1)}, bf16[128,256]{1,0:T(8,128)(2,1)S(1)}, u32[]{:S(2)}, u32[]{:S(2)}) %collective-permute-start) | collective-permute-done | bytes 65568 | tf_op jit(solution)/shard_map/ppermute | solution.py:272
  39.5 0.5 %collective-permute-start.1 = (bf16[128,256]{1,0:T(8,128)(2,1)S(1)}, bf16[128,256]{1,0:T(8,128)(2,1)S(1)}, u32[]{:S(2)}, u32[]{:S(2)}) collective-permute-start(bf16[128,256]{1,0:T(8,128)(2,1)S(1)} %collective-permute-done.near_ref), channel_id=1, source_target_pairs={{0,1},{1,0},{2,3},{3,2},{4,5},{5,4},{6,7},{7,6},{8,9},{9,8},{10,11... | collective-permute-start | bytes 196616 | tf_op jit(solution)/shard_map/ppermute | solution.py:274
  40.0 0.0 collective-permute-done.3.far_other_ref
  40.0 0.9 %collective-permute-done.1.near_other_ref = bf16[128,256]{1,0:T(8,128)(2,1)S(1)} collective-permute-done((bf16[128,256]{1,0:T(8,128)(2,1)S(1)}, bf16[128,256]{1,0:T(8,128)(2,1)S(1)}, u32[]{:S(2)}, u32[]{:S(2)}) %collective-permute-start.1) | collective-permute-done | bytes 65568 | tf_op jit(solution)/shard_map/ppermute | solution.py:274
  40.9 3.3 %correlate.1 = bf16[4,2,256,1024]{3,2,1,0:T(8,128)(2,1)} custom-call(bf16[128,256]{1,0:T(8,128)(2,1)S(1)} %arrange.1.rows_ref, bf16[128,256]{1,0:T(8,128)(2,1)S(1)} %collective-permute-done.near_ref, bf16[128,256]{1,0:T(8,128)(2,1)S(1)} %collective-permute-done.1.near_other_ref, bf16[128,256]{1,0:T(8,128)(2,1)S(1)} %collective-permute-done.2.far_ref, ...), custom_call_target="tpu_custom_call" | custom-call | tf_op jit(solution)/shard_map/correlate/pallas_call | solution.py:241
Async XLA Ops:
  27.3 8.0 %collective-permute-start.2 = (bf16[128,256]{1,0:T(8,128)(2,1)S(1)}, bf16[128,256]{1,0:T(8,128)(2,1)S(1)}, u32[]{:S(2)}, u32[]{:S(2)}) collective-permute-start(bf16[128,256]{1,0:T(8,128)(2,1)S(1)} %arrange.1.rows_ref), channel_id=1, source_target_pairs={{128,2},{130,0},{64,6},{66,4},{0,10},{2,8},{192,14},{194,12},{4,66... | collective-permute-start | bytes 196616 | tf_op jit(solution)/shard_map/ppermute | solution.py:273
  29.3 10.3 %collective-permute-start = (bf16[128,256]{1,0:T(8,128)(2,1)S(1)}, bf16[128,256]{1,0:T(8,128)(2,1)S(1)}, u32[]{:S(2)}, u32[]{:S(2)}) collective-permute-start(bf16[128,256]{1,0:T(8,128)(2,1)S(1)} %arrange.1.rows_ref), channel_id=1, source_target_pairs={{128,0},{64,4},{0,8},{192,12},{4,64},{196,68},{132,72},{68,76},{13... | collective-permute-start | bytes 196616 | tf_op jit(solution)/shard_map/ppermute | solution.py:272
  35.4 4.7 %collective-permute-start.3 = (bf16[128,256]{1,0:T(8,128)(2,1)S(1)}, bf16[128,256]{1,0:T(8,128)(2,1)S(1)}, u32[]{:S(2)}, u32[]{:S(2)}) collective-permute-start(bf16[128,256]{1,0:T(8,128)(2,1)S(1)} %collective-permute-done.2.far_ref), channel_id=1, source_target_pairs={{0,1},{1,0},{2,3},{3,2},{4,5},{5,4},{6,7},{7,6},{8,9},{9,8},{10,11... | collective-permute-start | bytes 196616 | tf_op jit(solution)/shard_map/ppermute | solution.py:275
  39.5 1.4 %collective-permute-start.1 = (bf16[128,256]{1,0:T(8,128)(2,1)S(1)}, bf16[128,256]{1,0:T(8,128)(2,1)S(1)}, u32[]{:S(2)}, u32[]{:S(2)}) collective-permute-start(bf16[128,256]{1,0:T(8,128)(2,1)S(1)} %collective-permute-done.near_ref), channel_id=1, source_target_pairs={{0,1},{1,0},{2,3},{3,2},{4,5},{5,4},{6,7},{7,6},{8,9},{9,8},{10,11... | collective-permute-start | bytes 196616 | tf_op jit(solution)/shard_map/ppermute | solution.py:274

commit v3 on v2

--- a/solution.py
+++ b/solution.py
@@ -15,19 +15,11 @@
 ROWS = 32
 HALF = 64
 VMEM_LIMIT = 60 * 2**20
-ARR_LIMIT = 16 * 2**20
-CORR_LIMIT = 16 * 2**20
+SMALL_LIMIT = 16 * 2**20
 
 
 AXES = ("x", "zh", "y", "zl", "co")
-
-
-def first_z():
-    return 2 * lax.axis_index("zl") + lax.axis_index("co")
-
-
-def first_x():
-    return lax.axis_index("y")
+FIRST = 2
 
 
 def exchange_groups():
@@ -35,7 +27,7 @@
     for y in range(4):
         for zl in range(2):
             for co in range(2):
-                members = [((p + y) % 4, (q + 2 * zl + co) % 4) for q in range(4) for p in range(4)]
+                members = [((p + FIRST) % 4, (q + FIRST) % 4) for q in range(4) for p in range(4)]
                 groups.append([(((x * 4 + z) * 4 + y) * 2 + zl) * 2 + co for x, z in members])
     return groups
 
@@ -134,7 +126,7 @@
         rows = slice(c * 8, (c + 1) * 8)
         piece = [part[rows, at : at + LANES] for part in (own, after) for at in (0, LANES)]
         piece = jnp.concatenate(piece, axis=0)
-        place = (c - first_z()) % 4
+        place = (c - FIRST) % 4
         for x in range(4):
             out_ref[place * 4 + x] = piece
 
@@ -167,11 +159,9 @@
 def arrange_kernel(got_ref, rows_ref):
     low = lax.broadcasted_iota(jnp.int32, (8, LANES), 1) < HALF
 
-    turn_x, turn_z = first_x(), first_z()
-
     def spectra(x, col, late):
         def part(x, at):
-            place = (col - turn_z) % 4 * 4 + (x - turn_x) % 4
+            place = (col - FIRST) % 4 * 4 + (x - FIRST) % 4
             return got_ref[place, pl.ds(at, 8)]
 
         total = part(x, 8 * late)
@@ -198,7 +188,7 @@
     return pl.pallas_call(
         arrange_kernel,
         out_shape=jax.ShapeDtypeStruct((LANES, 256), jnp.bfloat16),
-        compiler_params=pltpu.CompilerParams(vmem_limit_bytes=ARR_LIMIT),
+        compiler_params=pltpu.CompilerParams(vmem_limit_bytes=SMALL_LIMIT),
         name="arrange",
     )(got)
 
@@ -224,15 +214,12 @@
     def copy(k):
         return pltpu.make_async_copy(held_ref.at[k], out_ref.at[k // 2, k % 2], sem.at[k])
 
-    @pl.loop(0, 8)
-    def _(k):
+    for k in range(8):
         chosen = jnp.where(lane % 4 == k // 2, left_ref[k % 2], 0.0).astype(jnp.bfloat16)
         product = jnp.dot(chosen, right_ref[...], preferred_element_type=jnp.float32)
         held_ref[k] = (product * scale).astype(jnp.bfloat16)
         copy(k).start()
-
-    @pl.loop(0, 8)
-    def _(k):
+    for k in range(8):
         copy(k).wait()
 
 
@@ -249,12 +236,12 @@
             pltpu.VMEM((8, width, 4 * width), jnp.bfloat16),
             pltpu.SemaphoreType.DMA((8,)),
         ],
-        compiler_params=pltpu.CompilerParams(vmem_limit_bytes=CORR_LIMIT),
+        compiler_params=pltpu.CompilerParams(vmem_limit_bytes=SMALL_LIMIT),
         name="correlate",
     )(rows, *blocks)
 
 
-def across():
+def across_near():
     pairs = []
     for x in range(4):
         for y in range(4):
@@ -263,13 +250,22 @@
     return pairs
 
 
+def across_far():
+    pairs = []
+    for x in range(4):
+        for y in range(4):
+            source = (x + 2 + (y - x)) % 4
+            pairs.append((source * 4 + x, x * 4 + y))
+    return pairs
+
+
 def shards(voltages, taps, channels):
     pieces = filterbank(voltages, taps, channels)
     got = lax.all_to_all(pieces, AXES, 0, 0, axis_index_groups=exchange_groups(), tiled=True)
     rows = arrange(got)
     swap = [(0, 1), (1, 0)]
-    pairs = [(2 * s + z, 2 * d + 1 - z) for s, d in across() for z in range(2)]
-    near = lax.ppermute(rows, ("x", "y"), across())
+    pairs = [(2 * s + z, 2 * d + 1 - z) for s, d in across_far() for z in range(2)]
+    near = lax.ppermute(rows, ("x", "y"), across_near())
     far = lax.ppermute(rows, ("x", "y", "zl"), pairs)
     near_other = lax.ppermute(near, "co", swap)
     far_other = lax.ppermute(far, "co", swap)

time: 44.5 us -> 41.6 us (0.935)
  blocking collectives: 21 us -> 18.1 us
  starting transfers between devices: 7.1 us -> 9.3 us
  waiting for transfers between devices: 6.51 us -> 5.13 us
  Pallas kernels: 9.67 us -> 8.85 us
    ppermute x1, waiting for transfers between devices: 4.16 us -> 0.59 us  [shards(): far = lax.ppermute(rows, ('x', 'y', 'zl'), pairs)]
    all_to_all x1, blocking collectives: 21 us -> 18.1 us  [shards(): lax.all_to_all(pieces, AXES, 0, 0, axis_index_groups=exchange_groups(), t...]
    ppermute x1, waiting for transfers between devices: 1.44 us -> 3.64 us  [shards(): near = lax.ppermute(rows, ('x', 'y'), across_near())]
    ppermute x1, starting transfers between devices: 1.93 us -> 3.4 us  [shards(): near = lax.ppermute(rows, ('x', 'y'), across_near())]
    pallas_call x1, Pallas kernels: 3.34 us -> 2.54 us  [correlate(): pl.pallas_call(functools.partial(correlate_kernel, scale), in_specs=[pl.B...]
where the time goes in v3:
time: 41.6 us; the launch traced here: 41.4 us
  blocking collectives  18.1 us (44%)
  starting transfers between devices  9.3 us (22%)
  Pallas kernels  8.85 us (21%)
  waiting for transfers between devices  5.13 us (12%)
    all_to_all x1, blocking collectives, shards(): lax.all_to_all(pieces, AXES, 0, 0, axis_index_groups=exchange_groups(), t...  18.1 us
    pallas_call x1, Pallas kernels, filterbank(): pl.pallas_call(filterbank_kernel, in_specs=[pl.BlockSpec(memory_space=plt...  6.23 us
    ppermute x1, waiting for transfers between devices, shards(): near = lax.ppermute(rows, ('x', 'y'), across_near())  3.64 us
    ppermute x1, starting transfers between devices, shards(): near = lax.ppermute(rows, ('x', 'y'), across_near())  3.4 us
    ppermute x1, starting transfers between devices, shards(): far_other = lax.ppermute(far, 'co', swap)  2.98 us
    pallas_call x1, Pallas kernels, correlate(): pl.pallas_call(functools.partial(correlate_kernel, scale), in_specs=[pl.B...  2.54 us
    ppermute x1, starting transfers between devices, shards(): far = lax.ppermute(rows, ('x', 'y', 'zl'), pairs)  2.31 us
    ppermute x1, waiting for transfers between devices, shards(): near_other = lax.ppermute(near, 'co', swap)  0.9 us
  transfers between devices with their start and end apart: 4, of which 3 were waited for; matrix products, arithmetic and copies ran while one was open for 0% of the time, Pallas kernels for 0%

profile of v3, /device:TPU:7, one launch (start us, length us, event | category | flops | bytes accessed | tf_op | source)
XLA Modules:
  0.0 41.4 jit_solution(9817778197501190115)
XLA Ops:
  0.0 6.2 %filterbank.1 = f32[16,32,128]{2,1,0:T(8,128)} custom-call(s32[16]{0:T(128)} %chan_ref.1, bf16[64,65536]{1,0:T(8,128)(2,1)} %volt_ref.1, f32[4,16384]{1,0:T(4,128)} %taps_ref.1), custom_call_target="tpu_custom_call" | custom-call | tf_op jit(solution)/shard_map/filterbank/pallas_call | solution.py:136
  6.2 18.1 %all_to_all.5.got_ref = f32[16,32,128]{2,1,0:T(8,128)S(1)} all-to-all(f32[16,32,128]{2,1,0:T(8,128)} %filterbank.1), channel_id=1, replica_groups={{160,224,32,96,176,240,48,112,128,192,0,64,144,208,16,80},{161,225,33,9..., dimensions={0} | all-to-all | bytes 524288 | tf_op jit(solution)/shard_map/all_to_all | solution.py:264
  24.4 0.1 arrange.1.rows_ref
  24.5 2.3 %collective-permute-start.2 = (bf16[128,256]{1,0:T(8,128)(2,1)S(1)}, bf16[128,256]{1,0:T(8,128)(2,1)S(1)}, u32[]{:S(2)}, u32[]{:S(2)}) collective-permute-start(bf16[128,256]{1,0:T(8,128)(2,1)S(1)} %arrange.1.rows_ref), channel_id=1, source_target_pairs={{128,2},{130,0},{192,6},{194,4},{0,10},{2,8},{64,14},{66,12},{132,... | collective-permute-start | bytes 196616 | tf_op jit(solution)/shard_map/ppermute | solution.py:269
  26.8 3.4 %collective-permute-start = (bf16[128,256]{1,0:T(8,128)(2,1)S(1)}, bf16[128,256]{1,0:T(8,128)(2,1)S(1)}, u32[]{:S(2)}, u32[]{:S(2)}) collective-permute-start(bf16[128,256]{1,0:T(8,128)(2,1)S(1)} %arrange.1.rows_ref), channel_id=1, source_target_pairs={{128,0},{64,4},{0,8},{192,12},{4,64},{196,68},{132,72},{68,76},{13... | collective-permute-start | bytes 196616 | tf_op jit(solution)/shard_map/ppermute | solution.py:268
  30.2 0.6 %collective-permute-done.2.far_ref = bf16[128,256]{1,0:T(8,128)(2,1)S(1)} collective-permute-done((bf16[128,256]{1,0:T(8,128)(2,1)S(1)}, bf16[128,256]{1,0:T(8,128)(2,1)S(1)}, u32[]{:S(2)}, u32[]{:S(2)}) %collective-permute-start.2) | collective-permute-done | bytes 65568 | tf_op jit(solution)/shard_map/ppermute | solution.py:269
  30.8 3.0 %collective-permute-start.3 = (bf16[128,256]{1,0:T(8,128)(2,1)S(1)}, bf16[128,256]{1,0:T(8,128)(2,1)S(1)}, u32[]{:S(2)}, u32[]{:S(2)}) collective-permute-start(bf16[128,256]{1,0:T(8,128)(2,1)S(1)} %collective-permute-done.2.far_ref), channel_id=1, source_target_pairs={{0,1},{1,0},{2,3},{3,2},{4,5},{5,4},{6,7},{7,6},{8,9},{9,8},{10,11... | collective-permute-start | bytes 196616 | tf_op jit(solution)/shard_map/ppermute | solution.py:271
  33.7 3.6 %collective-permute-done.near_ref = bf16[128,256]{1,0:T(8,128)(2,1)S(1)} collective-permute-done((bf16[128,256]{1,0:T(8,128)(2,1)S(1)}, bf16[128,256]{1,0:T(8,128)(2,1)S(1)}, u32[]{:S(2)}, u32[]{:S(2)}) %collective-permute-start) | collective-permute-done | bytes 65568 | tf_op jit(solution)/shard_map/ppermute | solution.py:268
  37.4 0.6 %collective-permute-start.1 = (bf16[128,256]{1,0:T(8,128)(2,1)S(1)}, bf16[128,256]{1,0:T(8,128)(2,1)S(1)}, u32[]{:S(2)}, u32[]{:S(2)}) collective-permute-start(bf16[128,256]{1,0:T(8,128)(2,1)S(1)} %collective-permute-done.near_ref), channel_id=1, source_target_pairs={{0,1},{1,0},{2,3},{3,2},{4,5},{5,4},{6,7},{7,6},{8,9},{9,8},{10,11... | collective-permute-start | bytes 196616 | tf_op jit(solution)/shard_map/ppermute | solution.py:270
  38.0 0.0 collective-permute-done.3.far_other_ref
  38.0 0.9 %collective-permute-done.1.near_other_ref = bf16[128,256]{1,0:T(8,128)(2,1)S(1)} collective-permute-done((bf16[128,256]{1,0:T(8,128)(2,1)S(1)}, bf16[128,256]{1,0:T(8,128)(2,1)S(1)}, u32[]{:S(2)}, u32[]{:S(2)}) %collective-permute-start.1) | collective-permute-done | bytes 65568 | tf_op jit(solution)/shard_map/ppermute | solution.py:270
  38.9 2.5 %correlate.1 = bf16[4,2,256,1024]{3,2,1,0:T(8,128)(2,1)} custom-call(bf16[128,256]{1,0:T(8,128)(2,1)S(1)} %arrange.1.rows_ref, bf16[128,256]{1,0:T(8,128)(2,1)S(1)} %collective-permute-done.near_ref, bf16[128,256]{1,0:T(8,128)(2,1)S(1)} %collective-permute-done.1.near_other_ref, bf16[128,256]{1,0:T(8,128)(2,1)S(1)} %collective-permute-done.2.far_ref, ...), custom_call_target="tpu_custom_call" | custom-call | tf_op jit(solution)/shard_map/correlate/pallas_call | solution.py:228
Async XLA Ops:
  24.5 6.3 %collective-permute-start.2 = (bf16[128,256]{1,0:T(8,128)(2,1)S(1)}, bf16[128,256]{1,0:T(8,128)(2,1)S(1)}, u32[]{:S(2)}, u32[]{:S(2)}) collective-permute-start(bf16[128,256]{1,0:T(8,128)(2,1)S(1)} %arrange.1.rows_ref), channel_id=1, source_target_pairs={{128,2},{130,0},{192,6},{194,4},{0,10},{2,8},{64,14},{66,12},{132,... | collective-permute-start | bytes 196616 | tf_op jit(solution)/shard_map/ppermute | solution.py:269
  26.8 10.6 %collective-permute-start = (bf16[128,256]{1,0:T(8,128)(2,1)S(1)}, bf16[128,256]{1,0:T(8,128)(2,1)S(1)}, u32[]{:S(2)}, u32[]{:S(2)}) collective-permute-start(bf16[128,256]{1,0:T(8,128)(2,1)S(1)} %arrange.1.rows_ref), channel_id=1, source_target_pairs={{128,0},{64,4},{0,8},{192,12},{4,64},{196,68},{132,72},{68,76},{13... | collective-permute-start | bytes 196616 | tf_op jit(solution)/shard_map/ppermute | solution.py:268
  30.8 7.2 %collective-permute-start.3 = (bf16[128,256]{1,0:T(8,128)(2,1)S(1)}, bf16[128,256]{1,0:T(8,128)(2,1)S(1)}, u32[]{:S(2)}, u32[]{:S(2)}) collective-permute-start(bf16[128,256]{1,0:T(8,128)(2,1)S(1)} %collective-permute-done.2.far_ref), channel_id=1, source_target_pairs={{0,1},{1,0},{2,3},{3,2},{4,5},{5,4},{6,7},{7,6},{8,9},{9,8},{10,11... | collective-permute-start | bytes 196616 | tf_op jit(solution)/shard_map/ppermute | solution.py:271
  37.4 1.5 %collective-permute-start.1 = (bf16[128,256]{1,0:T(8,128)(2,1)S(1)}, bf16[128,256]{1,0:T(8,128)(2,1)S(1)}, u32[]{:S(2)}, u32[]{:S(2)}) collective-permute-start(bf16[128,256]{1,0:T(8,128)(2,1)S(1)} %collective-permute-done.near_ref), channel_id=1, source_target_pairs={{0,1},{1,0},{2,3},{3,2},{4,5},{5,4},{6,7},{7,6},{8,9},{9,8},{10,11... | collective-permute-start | bytes 196616 | tf_op jit(solution)/shard_map/ppermute | solution.py:270

commit v4 on v3

--- a/solution.py
+++ b/solution.py
@@ -19,7 +19,8 @@
 
 
 AXES = ("x", "zh", "y", "zl", "co")
-FIRST = 2
+Z_ORDER = (2, 0, 3, 1)
+X_ORDER = (2, 3, 0, 1)
 
 
 def exchange_groups():
@@ -27,7 +28,7 @@
     for y in range(4):
         for zl in range(2):
             for co in range(2):
-                members = [((p + FIRST) % 4, (q + FIRST) % 4) for q in range(4) for p in range(4)]
+                members = [(x, z) for z in Z_ORDER for x in X_ORDER]
                 groups.append([(((x * 4 + z) * 4 + y) * 2 + zl) * 2 + co for x, z in members])
     return groups
 
@@ -126,7 +127,7 @@
         rows = slice(c * 8, (c + 1) * 8)
         piece = [part[rows, at : at + LANES] for part in (own, after) for at in (0, LANES)]
         piece = jnp.concatenate(piece, axis=0)
-        place = (c - FIRST) % 4
+        place = Z_ORDER.index(c)
         for x in range(4):
             out_ref[place * 4 + x] = piece
 
@@ -161,7 +162,7 @@
 
     def spectra(x, col, late):
         def part(x, at):
-            place = (col - FIRST) % 4 * 4 + (x - FIRST) % 4
+            place = Z_ORDER.index(col) * 4 + X_ORDER.index(x)
             return got_ref[place, pl.ds(at, 8)]
 
         total = part(x, 8 * late)

time: 41.6 us -> 41.2 us (level)
  starting transfers between devices: 9.3 us -> 13.1 us
  waiting for transfers between devices: 5.13 us -> 1.48 us
  blocking collectives: 18.1 us -> 17.6 us
    ppermute x1, waiting for transfers between devices: 3.64 us -> 0.14 us  [shards(): near = lax.ppermute(rows, ('x', 'y'), across_near())]
    ppermute x1, starting transfers between devices: 0.61 us -> 3.62 us  [shards(): near_other = lax.ppermute(near, 'co', swap)]
    ppermute x1, starting transfers between devices: 2.98 us -> 3.58 us  [shards(): far_other = lax.ppermute(far, 'co', swap)]
    all_to_all x1, blocking collectives: 18.1 us -> 17.6 us  [shards(): lax.all_to_all(pieces, AXES, 0, 0, axis_index_groups=exchange_groups(), t...]
where the time goes in v4:
time: 41.2 us; the launch traced here: 41 us
  blocking collectives  17.6 us (43%)
  starting transfers between devices  13.1 us (32%)
  Pallas kernels  8.85 us (21%)
  waiting for transfers between devices  1.48 us (4%)
    all_to_all x1, blocking collectives, shards(): lax.all_to_all(pieces, AXES, 0, 0, axis_index_groups=exchange_groups(), t...  17.6 us
    pallas_call x1, Pallas kernels, filterbank(): pl.pallas_call(filterbank_kernel, in_specs=[pl.BlockSpec(memory_space=plt...  6.23 us
    ppermute x1, starting transfers between devices, shards(): near = lax.ppermute(rows, ('x', 'y'), across_near())  3.69 us
    ppermute x1, starting transfers between devices, shards(): near_other = lax.ppermute(near, 'co', swap)  3.62 us
    ppermute x1, starting transfers between devices, shards(): far_other = lax.ppermute(far, 'co', swap)  3.58 us
    pallas_call x1, Pallas kernels, correlate(): pl.pallas_call(functools.partial(correlate_kernel, scale), in_specs=[pl.B...  2.54 us
    ppermute x1, starting transfers between devices, shards(): far = lax.ppermute(rows, ('x', 'y', 'zl'), pairs)  2.18 us
    ppermute x1, waiting for transfers between devices, shards(): near_other = lax.ppermute(near, 'co', swap)  0.9 us
  transfers between devices with their start and end apart: 4, of which 3 were waited for; matrix products, arithmetic and copies ran while one was open for 0% of the time, Pallas kernels for 0%

profile of v4, /device:TPU:7, one launch (start us, length us, event | category | flops | bytes accessed | tf_op | source)
XLA Modules:
  0.0 41.0 jit_solution(5948508537018544972)
XLA Ops:
  0.0 6.2 %filterbank.1 = f32[16,32,128]{2,1,0:T(8,128)} custom-call(s32[16]{0:T(128)} %chan_ref.1, bf16[64,65536]{1,0:T(8,128)(2,1)} %volt_ref.1, f32[4,16384]{1,0:T(4,128)} %taps_ref.1), custom_call_target="tpu_custom_call" | custom-call | tf_op jit(solution)/shard_map/filterbank/pallas_call | solution.py:137
  6.2 17.6 %all_to_all.5.got_ref = f32[16,32,128]{2,1,0:T(8,128)S(1)} all-to-all(f32[16,32,128]{2,1,0:T(8,128)} %filterbank.1), channel_id=1, replica_groups={{160,224,32,96,128,192,0,64,176,240,48,112,144,208,16,80},{161,225,33,9..., dimensions={0} | all-to-all | bytes 524288 | tf_op jit(solution)/shard_map/all_to_all | solution.py:265
  23.8 0.1 arrange.1.rows_ref
  23.9 2.2 %collective-permute-start.2 = (bf16[128,256]{1,0:T(8,128)(2,1)S(1)}, bf16[128,256]{1,0:T(8,128)(2,1)S(1)}, u32[]{:S(2)}, u32[]{:S(2)}) collective-permute-start(bf16[128,256]{1,0:T(8,128)(2,1)S(1)} %arrange.1.rows_ref), channel_id=1, source_target_pairs={{128,2},{130,0},{192,6},{194,4},{0,10},{2,8},{64,14},{66,12},{132,... | collective-permute-start | bytes 196616 | tf_op jit(solution)/shard_map/ppermute | solution.py:270
  26.1 3.7 %collective-permute-start = (bf16[128,256]{1,0:T(8,128)(2,1)S(1)}, bf16[128,256]{1,0:T(8,128)(2,1)S(1)}, u32[]{:S(2)}, u32[]{:S(2)}) collective-permute-start(bf16[128,256]{1,0:T(8,128)(2,1)S(1)} %arrange.1.rows_ref), channel_id=1, source_target_pairs={{128,0},{64,4},{0,8},{192,12},{4,64},{196,68},{132,72},{68,76},{13... | collective-permute-start | bytes 196616 | tf_op jit(solution)/shard_map/ppermute | solution.py:269
  29.8 0.4 %collective-permute-done.2.far_ref = bf16[128,256]{1,0:T(8,128)(2,1)S(1)} collective-permute-done((bf16[128,256]{1,0:T(8,128)(2,1)S(1)}, bf16[128,256]{1,0:T(8,128)(2,1)S(1)}, u32[]{:S(2)}, u32[]{:S(2)}) %collective-permute-start.2) | collective-permute-done | bytes 65568 | tf_op jit(solution)/shard_map/ppermute | solution.py:270
  30.2 3.6 %collective-permute-start.3 = (bf16[128,256]{1,0:T(8,128)(2,1)S(1)}, bf16[128,256]{1,0:T(8,128)(2,1)S(1)}, u32[]{:S(2)}, u32[]{:S(2)}) collective-permute-start(bf16[128,256]{1,0:T(8,128)(2,1)S(1)} %collective-permute-done.2.far_ref), channel_id=1, source_target_pairs={{0,1},{1,0},{2,3},{3,2},{4,5},{5,4},{6,7},{7,6},{8,9},{9,8},{10,11... | collective-permute-start | bytes 196616 | tf_op jit(solution)/shard_map/ppermute | solution.py:272
  33.8 0.1 collective-permute-done.near_ref
  34.0 3.6 %collective-permute-start.1 = (bf16[128,256]{1,0:T(8,128)(2,1)S(1)}, bf16[128,256]{1,0:T(8,128)(2,1)S(1)}, u32[]{:S(2)}, u32[]{:S(2)}) collective-permute-start(bf16[128,256]{1,0:T(8,128)(2,1)S(1)} %collective-permute-done.near_ref), channel_id=1, source_target_pairs={{0,1},{1,0},{2,3},{3,2},{4,5},{5,4},{6,7},{7,6},{8,9},{9,8},{10,11... | collective-permute-start | bytes 196616 | tf_op jit(solution)/shard_map/ppermute | solution.py:271
  37.6 0.0 collective-permute-done.3.far_other_ref
  37.6 0.9 %collective-permute-done.1.near_other_ref = bf16[128,256]{1,0:T(8,128)(2,1)S(1)} collective-permute-done((bf16[128,256]{1,0:T(8,128)(2,1)S(1)}, bf16[128,256]{1,0:T(8,128)(2,1)S(1)}, u32[]{:S(2)}, u32[]{:S(2)}) %collective-permute-start.1) | collective-permute-done | bytes 65568 | tf_op jit(solution)/shard_map/ppermute | solution.py:271
  38.5 2.5 %correlate.1 = bf16[4,2,256,1024]{3,2,1,0:T(8,128)(2,1)} custom-call(bf16[128,256]{1,0:T(8,128)(2,1)S(1)} %arrange.1.rows_ref, bf16[128,256]{1,0:T(8,128)(2,1)S(1)} %collective-permute-done.near_ref, bf16[128,256]{1,0:T(8,128)(2,1)S(1)} %collective-permute-done.1.near_other_ref, bf16[128,256]{1,0:T(8,128)(2,1)S(1)} %collective-permute-done.2.far_ref, ...), custom_call_target="tpu_custom_call" | custom-call | tf_op jit(solution)/shard_map/correlate/pallas_call | solution.py:229
Async XLA Ops:
  23.9 6.3 %collective-permute-start.2 = (bf16[128,256]{1,0:T(8,128)(2,1)S(1)}, bf16[128,256]{1,0:T(8,128)(2,1)S(1)}, u32[]{:S(2)}, u32[]{:S(2)}) collective-permute-start(bf16[128,256]{1,0:T(8,128)(2,1)S(1)} %arrange.1.rows_ref), channel_id=1, source_target_pairs={{128,2},{130,0},{192,6},{194,4},{0,10},{2,8},{64,14},{66,12},{132,... | collective-permute-start | bytes 196616 | tf_op jit(solution)/shard_map/ppermute | solution.py:270
  26.1 7.8 %collective-permute-start = (bf16[128,256]{1,0:T(8,128)(2,1)S(1)}, bf16[128,256]{1,0:T(8,128)(2,1)S(1)}, u32[]{:S(2)}, u32[]{:S(2)}) collective-permute-start(bf16[128,256]{1,0:T(8,128)(2,1)S(1)} %arrange.1.rows_ref), channel_id=1, source_target_pairs={{128,0},{64,4},{0,8},{192,12},{4,64},{196,68},{132,72},{68,76},{13... | collective-permute-start | bytes 196616 | tf_op jit(solution)/shard_map/ppermute | solution.py:269
  30.2 7.4 %collective-permute-start.3 = (bf16[128,256]{1,0:T(8,128)(2,1)S(1)}, bf16[128,256]{1,0:T(8,128)(2,1)S(1)}, u32[]{:S(2)}, u32[]{:S(2)}) collective-permute-start(bf16[128,256]{1,0:T(8,128)(2,1)S(1)} %collective-permute-done.2.far_ref), channel_id=1, source_target_pairs={{0,1},{1,0},{2,3},{3,2},{4,5},{5,4},{6,7},{7,6},{8,9},{9,8},{10,11... | collective-permute-start | bytes 196616 | tf_op jit(solution)/shard_map/ppermute | solution.py:272
  34.0 4.5 %collective-permute-start.1 = (bf16[128,256]{1,0:T(8,128)(2,1)S(1)}, bf16[128,256]{1,0:T(8,128)(2,1)S(1)}, u32[]{:S(2)}, u32[]{:S(2)}) collective-permute-start(bf16[128,256]{1,0:T(8,128)(2,1)S(1)} %collective-permute-done.near_ref), channel_id=1, source_target_pairs={{0,1},{1,0},{2,3},{3,2},{4,5},{5,4},{6,7},{7,6},{8,9},{9,8},{10,11... | collective-permute-start | bytes 196616 | tf_op jit(solution)/shard_map/ppermute | solution.py:271

commit v5 on v4

--- a/solution.py
+++ b/solution.py
@@ -205,10 +205,8 @@
     width = near_ref.shape[1]
     mine = 2 * lax.axis_index("zl") + lax.axis_index("co")
     for k, block in enumerate((near_ref, near_other_ref, far_ref, far_other_ref)):
-        for place in range(4):
-            @pl.when(mine == place ^ k)
-            def _():
-                right_ref[:, place * width : (place + 1) * width] = block[...]
+        column = pl.multiple_of((mine ^ k) * width, width)
+        right_ref[:, pl.ds(column, width)] = block[...]
 
     lane = lax.broadcasted_iota(jnp.int32, left_ref.shape[1:], 1)
 

time: 41.2 us -> 41.1 us (level)
  no operation moved by 1% of the time
where the time goes in v5:
time: 41.1 us; the launch traced here: 40.9 us
  blocking collectives  17.6 us (43%)
  starting transfers between devices  13.1 us (32%)
  Pallas kernels  8.74 us (21%)
  waiting for transfers between devices  1.48 us (4%)
    all_to_all x1, blocking collectives, shards(): lax.all_to_all(pieces, AXES, 0, 0, axis_index_groups=exchange_groups(), t...  17.6 us
    pallas_call x1, Pallas kernels, filterbank(): pl.pallas_call(filterbank_kernel, in_specs=[pl.BlockSpec(memory_space=plt...  6.23 us
    ppermute x1, starting transfers between devices, shards(): near = lax.ppermute(rows, ('x', 'y'), across_near())  3.69 us
    ppermute x1, starting transfers between devices, shards(): near_other = lax.ppermute(near, 'co', swap)  3.62 us
    ppermute x1, starting transfers between devices, shards(): far_other = lax.ppermute(far, 'co', swap)  3.58 us
    pallas_call x1, Pallas kernels, correlate(): pl.pallas_call(functools.partial(correlate_kernel, scale), in_specs=[pl.B...  2.42 us
    ppermute x1, starting transfers between devices, shards(): far = lax.ppermute(rows, ('x', 'y', 'zl'), pairs)  2.18 us
    ppermute x1, waiting for transfers between devices, shards(): near_other = lax.ppermute(near, 'co', swap)  0.9 us
  transfers between devices with their start and end apart: 4, of which 3 were waited for; matrix products, arithmetic and copies ran while one was open for 0% of the time, Pallas kernels for 0%

profile of v5, /device:TPU:7, one launch (start us, length us, event | category | flops | bytes accessed | tf_op | source)
XLA Modules:
  0.0 40.9 jit_solution(50936397201363703)
XLA Ops:
  0.0 6.2 %filterbank.1 = f32[16,32,128]{2,1,0:T(8,128)} custom-call(s32[16]{0:T(128)} %chan_ref.1, bf16[64,65536]{1,0:T(8,128)(2,1)} %volt_ref.1, f32[4,16384]{1,0:T(4,128)} %taps_ref.1), custom_call_target="tpu_custom_call" | custom-call | tf_op jit(solution)/shard_map/filterbank/pallas_call | solution.py:137
  6.2 17.6 %all_to_all.5.got_ref = f32[16,32,128]{2,1,0:T(8,128)S(1)} all-to-all(f32[16,32,128]{2,1,0:T(8,128)} %filterbank.1), channel_id=1, replica_groups={{160,224,32,96,128,192,0,64,176,240,48,112,144,208,16,80},{161,225,33,9..., dimensions={0} | all-to-all | bytes 524288 | tf_op jit(solution)/shard_map/all_to_all | solution.py:263
  23.8 0.1 arrange.1.rows_ref
  23.9 2.2 %collective-permute-start.2 = (bf16[128,256]{1,0:T(8,128)(2,1)S(1)}, bf16[128,256]{1,0:T(8,128)(2,1)S(1)}, u32[]{:S(2)}, u32[]{:S(2)}) collective-permute-start(bf16[128,256]{1,0:T(8,128)(2,1)S(1)} %arrange.1.rows_ref), channel_id=1, source_target_pairs={{128,2},{130,0},{192,6},{194,4},{0,10},{2,8},{64,14},{66,12},{132,... | collective-permute-start | bytes 196616 | tf_op jit(solution)/shard_map/ppermute | solution.py:268
  26.1 3.7 %collective-permute-start = (bf16[128,256]{1,0:T(8,128)(2,1)S(1)}, bf16[128,256]{1,0:T(8,128)(2,1)S(1)}, u32[]{:S(2)}, u32[]{:S(2)}) collective-permute-start(bf16[128,256]{1,0:T(8,128)(2,1)S(1)} %arrange.1.rows_ref), channel_id=1, source_target_pairs={{128,0},{64,4},{0,8},{192,12},{4,64},{196,68},{132,72},{68,76},{13... | collective-permute-start | bytes 196616 | tf_op jit(solution)/shard_map/ppermute | solution.py:267
  29.8 0.4 %collective-permute-done.2.far_ref = bf16[128,256]{1,0:T(8,128)(2,1)S(1)} collective-permute-done((bf16[128,256]{1,0:T(8,128)(2,1)S(1)}, bf16[128,256]{1,0:T(8,128)(2,1)S(1)}, u32[]{:S(2)}, u32[]{:S(2)}) %collective-permute-start.2) | collective-permute-done | bytes 65568 | tf_op jit(solution)/shard_map/ppermute | solution.py:268
  30.2 3.6 %collective-permute-start.3 = (bf16[128,256]{1,0:T(8,128)(2,1)S(1)}, bf16[128,256]{1,0:T(8,128)(2,1)S(1)}, u32[]{:S(2)}, u32[]{:S(2)}) collective-permute-start(bf16[128,256]{1,0:T(8,128)(2,1)S(1)} %collective-permute-done.2.far_ref), channel_id=1, source_target_pairs={{0,1},{1,0},{2,3},{3,2},{4,5},{5,4},{6,7},{7,6},{8,9},{9,8},{10,11... | collective-permute-start | bytes 196616 | tf_op jit(solution)/shard_map/ppermute | solution.py:270
  33.8 0.1 collective-permute-done.near_ref
  34.0 3.6 %collective-permute-start.1 = (bf16[128,256]{1,0:T(8,128)(2,1)S(1)}, bf16[128,256]{1,0:T(8,128)(2,1)S(1)}, u32[]{:S(2)}, u32[]{:S(2)}) collective-permute-start(bf16[128,256]{1,0:T(8,128)(2,1)S(1)} %collective-permute-done.near_ref), channel_id=1, source_target_pairs={{0,1},{1,0},{2,3},{3,2},{4,5},{5,4},{6,7},{7,6},{8,9},{9,8},{10,11... | collective-permute-start | bytes 196616 | tf_op jit(solution)/shard_map/ppermute | solution.py:269
  37.6 0.0 collective-permute-done.3.far_other_ref
  37.6 0.9 %collective-permute-done.1.near_other_ref = bf16[128,256]{1,0:T(8,128)(2,1)S(1)} collective-permute-done((bf16[128,256]{1,0:T(8,128)(2,1)S(1)}, bf16[128,256]{1,0:T(8,128)(2,1)S(1)}, u32[]{:S(2)}, u32[]{:S(2)}) %collective-permute-start.1) | collective-permute-done | bytes 65568 | tf_op jit(solution)/shard_map/ppermute | solution.py:269
  38.5 2.4 %correlate.1 = bf16[4,2,256,1024]{3,2,1,0:T(8,128)(2,1)} custom-call(bf16[128,256]{1,0:T(8,128)(2,1)S(1)} %arrange.1.rows_ref, bf16[128,256]{1,0:T(8,128)(2,1)S(1)} %collective-permute-done.near_ref, bf16[128,256]{1,0:T(8,128)(2,1)S(1)} %collective-permute-done.1.near_other_ref, bf16[128,256]{1,0:T(8,128)(2,1)S(1)} %collective-permute-done.2.far_ref, ...), custom_call_target="tpu_custom_call" | custom-call | tf_op jit(solution)/shard_map/correlate/pallas_call | solution.py:227
Async XLA Ops:
  23.9 6.3 %collective-permute-start.2 = (bf16[128,256]{1,0:T(8,128)(2,1)S(1)}, bf16[128,256]{1,0:T(8,128)(2,1)S(1)}, u32[]{:S(2)}, u32[]{:S(2)}) collective-permute-start(bf16[128,256]{1,0:T(8,128)(2,1)S(1)} %arrange.1.rows_ref), channel_id=1, source_target_pairs={{128,2},{130,0},{192,6},{194,4},{0,10},{2,8},{64,14},{66,12},{132,... | collective-permute-start | bytes 196616 | tf_op jit(solution)/shard_map/ppermute | solution.py:268
  26.1 7.8 %collective-permute-start = (bf16[128,256]{1,0:T(8,128)(2,1)S(1)}, bf16[128,256]{1,0:T(8,128)(2,1)S(1)}, u32[]{:S(2)}, u32[]{:S(2)}) collective-permute-start(bf16[128,256]{1,0:T(8,128)(2,1)S(1)} %arrange.1.rows_ref), channel_id=1, source_target_pairs={{128,0},{64,4},{0,8},{192,12},{4,64},{196,68},{132,72},{68,76},{13... | collective-permute-start | bytes 196616 | tf_op jit(solution)/shard_map/ppermute | solution.py:267
  30.2 7.4 %collective-permute-start.3 = (bf16[128,256]{1,0:T(8,128)(2,1)S(1)}, bf16[128,256]{1,0:T(8,128)(2,1)S(1)}, u32[]{:S(2)}, u32[]{:S(2)}) collective-permute-start(bf16[128,256]{1,0:T(8,128)(2,1)S(1)} %collective-permute-done.2.far_ref), channel_id=1, source_target_pairs={{0,1},{1,0},{2,3},{3,2},{4,5},{5,4},{6,7},{7,6},{8,9},{9,8},{10,11... | collective-permute-start | bytes 196616 | tf_op jit(solution)/shard_map/ppermute | solution.py:270
  34.0 4.5 %collective-permute-start.1 = (bf16[128,256]{1,0:T(8,128)(2,1)S(1)}, bf16[128,256]{1,0:T(8,128)(2,1)S(1)}, u32[]{:S(2)}, u32[]{:S(2)}) collective-permute-start(bf16[128,256]{1,0:T(8,128)(2,1)S(1)} %collective-permute-done.near_ref), channel_id=1, source_target_pairs={{0,1},{1,0},{2,3},{3,2},{4,5},{5,4},{6,7},{7,6},{8,9},{9,8},{10,11... | collective-permute-start | bytes 196616 | tf_op jit(solution)/shard_map/ppermute | solution.py:269
